TPU v7x, 32 devices: a whole 2x2x4 slice. The times are simulated.
32 devices in a mesh: replica: 2 (over core), fsdp: 4 (over y, x), tensor: 4 (over z).
Axes of the slice: x: 2, y: 2, z: 4, core: 2. Of those that a mesh axis runs over, the one named last changes fastest.
Arguments:
- grads: bfloat16 [2, 2, 4096, 14336], P('replica', None, 'fsdp', 'tensor'), may hold values from -6 to 6
- momentum: bfloat16 [2, 4096, 14336], P(None, 'fsdp', 'tensor'), may hold values from -50 to 50, as said below
- basis: bfloat16 [2, 14336, 512], P(None, 'tensor'), may hold values from -0.046875 to 0.046875
Outputs:
- momentum_new: bfloat16 [2, 4096, 14336], P(None, 'fsdp', 'tensor')
- update: bfloat16 [2, 4096, 14336], P(None, 'fsdp', 'tensor')
- basis_new: bfloat16 [2, 14336, 512], P(None, 'tensor')
Inputs may be any that keep to these rules, and one draw needn't show every extreme that they name: `momentum`: entries are finite.
All inputs are finite; a program needn't handle non-finite values.
Results may differ from a plain program's by a relative error of at most 0.028.
Values may be sent and summed in bfloat16 or wider, within the bound.
No kernel may reach another device: no remote copies, remote signals or barrier semaphores. Data moves between devices by JAX's collectives and lax.ppermute only.
A program may use at most 192 MiB of HBM per device.

v0:
```python
import math

import jax
import jax.numpy as jnp
from jax import lax
from jax.sharding import PartitionSpec as P

FEATURES = 4096
UNITS = 14336
RANK = 512


momentum_decay = 0.95


def orthonormal(projected, factor):

    def solve_one(lower_mat, rows_mat):
        return jax.scipy.linalg.solve_triangular(lower_mat, rows_mat.T, lower=True).T

    return jax.vmap(solve_one)(factor, projected).astype(jnp.bfloat16)


def full_back(blended, left_basis):
    back_piece = lax.psum_scatter(
        jnp.einsum("wmc,wmr->cwr", blended, left_basis, preferred_element_type=jnp.float32).astype(
            jnp.bfloat16
        ),
        "fsdp",
        scatter_dimension=0,
        tiled=True,
    ).astype(jnp.float32)
    squares = lax.psum(jnp.sum(back_piece * back_piece, axis=0), ("fsdp", "tensor"))
    back_b = back_piece.astype(jnp.bfloat16)
    right_rows = lax.all_gather(back_b, "fsdp", axis=0, tiled=True)
    return (squares, right_rows)


def power_step(total_grad, moment, right):
    blended = (moment.astype(jnp.float32) + total_grad).astype(jnp.bfloat16)
    partial_value = jnp.einsum("wmc,wcr->wmr", blended, right, preferred_element_type=jnp.float32)
    projected = lax.psum(partial_value.astype(jnp.bfloat16), "tensor").astype(jnp.float32)
    gram_local = jnp.einsum(
        "wmr,wms->wrs",
        projected,
        projected,
        preferred_element_type=jnp.float32,
        precision=lax.Precision.HIGHEST,
    )
    gram_matrix = lax.psum(gram_local.astype(jnp.bfloat16), "fsdp").astype(jnp.float32)
    factor = jnp.linalg.cholesky(gram_matrix)
    left_basis = orthonormal(projected, factor)
    squares, right_rows = full_back(blended, left_basis)
    inverse = 1.0 / (jnp.sqrt(squares) + 1e-06)
    normed = (right_rows.astype(jnp.float32) * inverse[None, :, :]).astype(jnp.bfloat16)
    feedback = jnp.einsum(
        "wmr,cwr->wmc", left_basis, right_rows, preferred_element_type=jnp.float32
    )
    momentum_new = (blended.astype(jnp.float32) - (1.0 - momentum_decay) * feedback).astype(
        jnp.bfloat16
    )
    scale = math.sqrt(FEATURES * UNITS / RANK)
    update = (
        scale * jnp.einsum("wmr,cwr->wmc", left_basis, normed, preferred_element_type=jnp.float32)
    ).astype(jnp.bfloat16)
    basis_new = jnp.transpose(normed, (1, 0, 2))
    return (momentum_new, update, basis_new)


def shards(grads, momentum, basis):
    swapped = lax.all_to_all(grads, "replica", split_axis=1, concat_axis=0, tiled=True)
    total_grad = jnp.sum(swapped.astype(jnp.float32), axis=0)
    owner_index = lax.axis_index("replica")
    moment = lax.dynamic_slice_in_dim(momentum, owner_index, 1, 0)
    right = lax.dynamic_slice_in_dim(basis, owner_index, 1, 0)
    outputs = power_step(total_grad, moment, right)
    momentum_new, update, basis_new = (
        lax.all_gather(outputs[0], "replica", axis=0, tiled=True),
        lax.all_gather(outputs[1], "replica", axis=0, tiled=True),
        lax.all_gather(outputs[2], "replica", axis=0, tiled=True),
    )
    return (momentum_new, update, basis_new)


def solution(mesh):
    placed = (
        P("replica", None, "fsdp", "tensor"),
        P(None, "fsdp", "tensor"),
        P(None, "tensor", None),
    )
    return jax.shard_map(
        shards,
        mesh=mesh,
        in_specs=placed,
        out_specs=(P(None, "fsdp", "tensor"), P(None, "fsdp", "tensor"), P(None, "tensor", None)),
        check_vma=False,
    )
```

profile of v0, /device:TPU:0, one launch (start us, length us, event | category | flops | bytes accessed | tf_op | source)
XLA Modules:
  0.0 545.9 jit_solution(3601725933567158803)
XLA Ops:
  7.2 9.0 %all-to-all-start = ((bf16[1,2,1024,3584]{3,2,0,1:T(8,128)(2,1)}), bf16[1,2,1024,3584]{3,2,0,1:T(8,128)(2,1)}, u32[]{:S(2)}, u32[]{:S(2)}) async-start(bf16[1,2,1024,3584]{3,2,0,1:T(8,128)(2,1)} %bitcast.222), calls=%async_computation | async-start | bytes 29360128 | tf_op jit(solution)/shard_map/all_to_all | solution.py:71
  16.3 11.9 %all-to-all-done = bf16[1,2,1024,3584]{3,2,0,1:T(8,128)(2,1)} async-done(((bf16[1,2,1024,3584]{3,2,0,1:T(8,128)(2,1)}), bf16[1,2,1024,3584]{3,2,0,1:T(8,128)(2,1)}, u32[]{:S(2)}, u32[]{:S(2)}) %all-to-all-start) | async-done | bytes 14680096 | tf_op jit(solution)/shard_map/all_to_all | solution.py:71
  28.2 14.8 %convert_reduce_fusion = f32[1024,3584]{1,0:T(8,128)} fusion(bf16[1,2,1024,3584]{3,2,0,1:T(8,128)(2,1)} %all-to-all-done), kind=kLoop, calls=%fused_computation.2 | loop fusion | flops 11010048 | bytes 29360128 | tf_op jit(solution)/shard_map/reduce_sum | solution.py:72
  43.0 8.1 %fusion.1 = bf16[1,1024,3584]{2,1,0:T(8,128)(2,1)S(1)} fusion(f32[1024,3584]{1,0:T(8,128)} %convert_reduce_fusion, bf16[2,1024,3584]{2,1,0:T(8,128)(2,1)} %param.4, s32[]{:T(128)S(6)} %select_n.8), kind=kLoop, calls=%fused_computation.6 | loop fusion | flops 11010048 | bytes 29360132 | tf_op jit(solution)/shard_map/convert_element_type | solution.py:40
  51.2 3.0 copy-done.1
  54.2 4.9 fusion.26
  59.2 54.6 %all-reduce.4.cloned.1.call-done = bf16[1,1024,512]{2,1,0:T(8,128)(2,1)} async-done(((bf16[1,1024,512]{2,1,0:T(8,128)(2,1)}), bf16[1,1024,512]{2,1,0:T(8,128)(2,1)}) %all-reduce.4.cloned.1.call-update) | async-done | bytes 1048592 | tf_op jit(solution)/shard_map/psum | solution.py:42
  113.8 3.2 fusion.31
  118.9 43.5 %all-reduce.6.cloned.1.call-done = bf16[1,512,512]{1,2,0:T(8,128)(2,1)} async-done(((bf16[1,512,512]{1,2,0:T(8,128)(2,1)}), bf16[1,512,512]{1,2,0:T(8,128)(2,1)}) %all-reduce.6.cloned.1.call-update) | async-done | bytes 524304 | tf_op jit(solution)/shard_map/psum | solution.py:50
  164.9 11.7 %custom-call.35 = f32[1,128,128]{2,1,0:T(8,128)S(1)} custom-call(f32[1,128,128]{2,1,0:T(8,128)S(1)} %cholesky.267), custom_call_target="Cholesky" | custom-call | tf_op jit(solution)/shard_map/jit(cholesky)/cholesky | solution.py:51
  177.8 9.8 %custom-call.36 = f32[1,1,128,128]{2,3,1,0:T(8,128)S(1)} custom-call(f32[1,1,128,128]{3,2,1,0:T(8,128)S(1)} %get-tuple-element.36), custom_call_target="InvertDiagBlocksLowerTriangular" | custom-call | tf_op jit(solution)/shard_map/jit(cholesky)/cholesky | solution.py:51
  188.9 11.7 %custom-call.37 = f32[1,128,128]{2,1,0:T(8,128)S(1)} custom-call(f32[1,128,128]{2,1,0:T(8,128)S(1)} %cholesky.271), custom_call_target="Cholesky" | custom-call | tf_op jit(solution)/shard_map/jit(cholesky)/cholesky | solution.py:51
  201.3 10.0 %custom-call.38 = f32[1,1,128,128]{2,3,1,0:T(8,128)S(1)} custom-call(f32[1,1,128,128]{3,2,1,0:T(8,128)S(1)} %get-tuple-element.33), custom_call_target="InvertDiagBlocksLowerTriangular" | custom-call | tf_op jit(solution)/shard_map/jit(cholesky)/cholesky | solution.py:51
  213.6 11.7 %custom-call.39 = f32[1,128,128]{2,1,0:T(8,128)S(1)} custom-call(f32[1,128,128]{2,1,0:T(8,128)S(1)} %cholesky.276), custom_call_target="Cholesky" | custom-call | tf_op jit(solution)/shard_map/jit(cholesky)/cholesky | solution.py:51
  225.9 9.8 %custom-call.40 = f32[1,1,128,128]{2,3,1,0:T(8,128)S(1)} custom-call(f32[1,1,128,128]{3,2,1,0:T(8,128)S(1)} %get-tuple-element.30), custom_call_target="InvertDiagBlocksLowerTriangular" | custom-call | tf_op jit(solution)/shard_map/jit(cholesky)/cholesky | solution.py:51
  238.2 11.7 %custom-call.41 = f32[1,128,128]{2,1,0:T(8,128)S(1)} custom-call(f32[1,128,128]{2,1,0:T(8,128)S(1)} %fusion.44), custom_call_target="Cholesky" | custom-call | tf_op jit(solution)/shard_map/jit(cholesky)/cholesky | solution.py:51
  257.9 11.7 %while.1 = (s32[]{:T(128)}, f32[1,512,512]{2,1,0:T(8,128)}, s32[4,2]{0,1:T(2,128)S(1)}, f32[4,1,128,128]{3,2,1,0:T(8,128)S(1)}, s32[]{:T(128)}) while((s32[]{:T(128)}, f32[1,512,512]{2,1,0:T(8,128)}, s32[4,2]{0,1:T(2,128)S(1)}, f32[4,1,128,128]{3,2,1,0:T(8,128)S(1)}, s32[]{:T(128)}) %tuple.36), condition=%wide.while_cond, body=%wide.while_body.sunk | while | flops 2 | bytes 131189 | solution.py:19
  269.6 39.9 %custom-call.42 = f32[1,4,128,128]{2,3,1,0:T(8,128)} custom-call(f32[1,4,128,128]{3,2,1,0:T(8,128)S(1)} %bitcast.236), custom_call_target="InvertDiagBlocksLowerTriangular" | custom-call | tf_op jit(solution)/shard_map/vmap(jit(_solve_triangular))/triangular_solve | solution.py:19
  318.3 3.7 fusion.36
  323.4 5.4 fusion.9
  328.8 5.9 %copy.26 = bf16[3584,512]{1,0:T(8,128)(2,1)} copy(bf16[3584,512]{0,1:T(8,128)(2,1)} %fusion.9) | data formatting | bytes 7340032
  334.9 48.2 %reduce-scatter.4.cloned.1.call-done = bf16[896,512]{1,0:T(8,128)(2,1)} async-done(((bf16[3584,512]{1,0:T(8,128)(2,1)}), bf16[896,512]{1,0:T(8,128)(2,1)}) %reduce-scatter.4.cloned.1.call-update) | async-done | bytes 917520
  386.9 41.5 %psum.23 = f32[1,512]{1,0:T(1,128)S(1)} all-reduce(f32[1,512]{1,0:T(1,128)S(1)} %bitcast.232), channel_id=1, replica_groups=mesh['replica'=2,'fsdp'=4,'tensor'=4] {'fsdp','tensor'}, use_global_device_ids=true, to_apply=%region_13.14 | all-reduce | flops 512 | bytes 4096 | tf_op jit(solution)/shard_map/psum | solution.py:33
  428.4 6.0 %all-gather.7.cloned.1.call-done = bf16[3584,1,512]{0,2,1:T(8,128)(2,1)} async-done(((bf16[896,1,512]{0,2,1:T(8,128)(2,1)}), bf16[3584,1,512]{0,2,1:T(8,128)(2,1)}) %all-gather.7.cloned.1.call-update) | async-done | bytes 3670032 | tf_op jit(solution)/shard_map/all_gather | solution.py:35
  434.4 4.9 multiply_convert_fusion.1
  440.4 8.2 %multiply_convert_fusion = bf16[1024,3584]{1,0:T(8,128)(2,1)} fusion(bf16[3584,1,512]{0,2,1:T(8,128)(2,1)} %multiply_convert_fusion.1, bf16[1,128,1024]{2,1,0:T(8,128)(2,1)S(1)} %copy-done.6, bf16[1,128,1024]{2,1,0:T(8,128)(2,1)S(1)} %copy-done.10, bf16[1,128,1024]{2,1,0:T(8,128)(2,1)S(1)} %copy-done.8, bf16[1,128,1024]{2,1,0:T(8,128)(2,1)S(1)} %get-tuple-element.43), kind=kOutput, calls=%fused_computation.7 | convolution fusion | flops 3769630720 | bytes 12058624 | tf_op jit(solution)/shard_map/wmr,cwr->wmc/dot_general | solution.py:64
  448.7 10.5 %fusion = bf16[1,1024,3584]{2,1,0:T(8,128)(2,1)} fusion(bf16[1,1024,3584]{2,1,0:T(8,128)(2,1)} %copy-done.1, bf16[3584,1,512]{0,2,1:T(8,128)(2,1)} %all-gather.7.cloned.1.call-done, bf16[1,128,1024]{2,1,0:T(8,128)(2,1)S(1)} %copy-done.6, bf16[1,128,1024]{2,1,0:T(8,128)(2,1)S(1)} %copy-done.10, bf16[1,128,1024]{2,1,0:T(8,128)(2,1)S(1)} %copy-done.8, ...), kind=kOutput, calls=%fused_computation.4 | convolution fusion | flops 3776970752 | bytes 19398656 | tf_op jit(solution)/shard_map/wmr,cwr->wmc/dot_general | solution.py:56
  459.2 10.5 %copy.23 = bf16[7168,1,512]{2,0,1:T(8,128)(2,1)} copy(bf16[7168,1,512]{0,2,1:T(8,128)(2,1)} %all-gather.13.cloned.1.call-done) | data formatting | bytes 14680064
  469.7 18.3 %all-gather.11.cloned.1.call-done = bf16[2048,3584]{1,0:T(8,128)(2,1)} async-done(((bf16[1024,3584]{1,0:T(8,128)(2,1)}), bf16[2048,3584]{1,0:T(8,128)(2,1)}) %all-gather.11.cloned.1.call-update) | async-done | bytes 14680080 | tf_op jit(solution)/shard_map/all_gather | solution.py:79
  488.0 30.4 %all-gather.9.cloned.1.call-done = bf16[2,1024,3584]{2,1,0:T(8,128)(2,1)} async-done(((bf16[1,1024,3584]{2,1,0:T(8,128)(2,1)}), bf16[2,1024,3584]{2,1,0:T(8,128)(2,1)}) %all-gather.9.cloned.1.call-update) | async-done | bytes 14680080 | tf_op jit(solution)/shard_map/all_gather | solution.py:78
  518.4 13.7 %copy.47 = bf16[2,1024,3584]{2,1,0:T(8,128)(2,1)} copy(bf16[2,1024,3584]{2,1,0:T(8,128)(2,1)} %all-gather.9.cloned.1.call-done) | data formatting | bytes 29360128
  533.4 5.5 %copy.48 = bf16[2,1024,3584]{2,1,0:T(8,128)(2,1)} copy(bf16[2,1024,3584]{2,1,0:T(8,128)(2,1)S(1)} %bitcast.223) | data formatting | bytes 29360128
  (93 shorter events, 46.4 us)
Async XLA Ops:
  7.2 21.0 %all-to-all-start = ((bf16[1,2,1024,3584]{3,2,0,1:T(8,128)(2,1)}), bf16[1,2,1024,3584]{3,2,0,1:T(8,128)(2,1)}, u32[]{:S(2)}, u32[]{:S(2)}) async-start(bf16[1,2,1024,3584]{3,2,0,1:T(8,128)(2,1)} %bitcast.222), calls=%async_computation | async-start | bytes 29360128 | tf_op jit(solution)/shard_map/all_to_all | solution.py:71
  16.2 97.6 %all-reduce.4.cloned.1.call-start = ((), (), s32[]{:S(2)}) async-start(), calls=%async_computation.2 | async-start | bytes 2097152 | tf_op jit(solution)/shard_map/psum | solution.py:42
  28.2 26.0 %slice-start.2 = ((s8[7340032]{0:T(1024)(128)(4,1)}), s8[3145728]{0:T(1024)(128)(4,1)S(1)}, s32[]{:S(2)}) async-start(s8[7340032]{0:T(1024)(128)(4,1)} %bitcast.234), calls=%async_computation.11 | async-start | bytes 6291456
  43.0 11.2 %slice-start.3 = ((s8[7340032]{0:T(1024)(128)(4,1)}), s8[4194304]{0:T(1024)(128)(4,1)S(1)}, s32[]{:S(2)}) async-start(s8[7340032]{0:T(1024)(128)(4,1)} %bitcast.234), calls=%async_computation.12 | async-start | bytes 8388608
  51.2 3.1 copy-start.1
  59.2 103.3 %all-reduce.6.cloned.1.call-start = ((), (), s32[]{:S(2)}) async-start(), calls=%async_computation.3 | async-start | bytes 1048576 | tf_op jit(solution)/shard_map/psum | solution.py:50
  113.8 3.5 copy-start.4
  117.0 266.2 %reduce-scatter.4.cloned.1.call-start = ((), (), s32[]{:S(2)}) async-start(), calls=%async_computation.8 | async-start | bytes 4587520
  164.9 70.9 %copy-start.3 = (f32[1,512,512]{2,1,0:T(8,128)}, f32[1,512,512]{2,1,0:T(8,128)S(1)}, u32[]{:S(2)}) copy-start(f32[1,512,512]{2,1,0:T(8,128)S(1)} %fusion.47) | copy-start | bytes 3145732
  236.6 86.8 %slice-start = ((s8[7340032]{0:T(1024)(128)(4,1)}), s8[3145728]{0:T(1024)(128)(4,1)S(1)}, s32[]{:S(2)}) async-start(s8[7340032]{0:T(1024)(128)(4,1)} %bitcast.228), calls=%async_computation.9 | async-start | bytes 6291456
  309.5 5.3 copy-start.2
  309.5 8.1 %copy-start.11 = (f32[1,4,128,128]{2,3,1,0:T(8,128)S(1)}, f32[1,4,128,128]{2,3,1,0:T(8,128)}, u32[]{:S(2)}) copy-start(f32[1,4,128,128]{2,3,1,0:T(8,128)} %custom-call.42) | copy-start | bytes 786436
  313.2 10.2 %slice-start.1 = ((s8[7340032]{0:T(1024)(128)(4,1)}), s8[4194304]{0:T(1024)(128)(4,1)S(1)}, s32[]{:S(2)}) async-start(s8[7340032]{0:T(1024)(128)(4,1)} %bitcast.228), calls=%async_computation.10 | async-start | bytes 8388608
  314.8 7.9 %copy-start.7 = (bf16[1,128,1024]{2,1,0:T(8,128)(2,1)}, bf16[1,128,1024]{2,1,0:T(8,128)(2,1)S(1)}, u32[]{:S(2)}) copy-start(bf16[1,128,1024]{2,1,0:T(8,128)(2,1)S(1)} %get-tuple-element.41) | copy-start | bytes 786436
  318.3 4.4 copy-start.9
  322.7 0.7 copy-start.5
  334.7 99.7 %all-gather.7.cloned.1.call-start = ((), (), s32[]{:S(2)}) async-start(), calls=%async_computation.4 | async-start | bytes 4587520 | tf_op jit(solution)/shard_map/all_gather | solution.py:35
  385.4 73.8 %all-gather.13.cloned.1.call-start = ((), (), s32[]{:S(2)}) async-start(), calls=%async_computation.7 | async-start | bytes 11010048 | tf_op jit(solution)/shard_map/all_gather | solution.py:80
  439.3 0.9 copy-start.6
  439.3 1.0 copy-start.8
  439.3 1.1 copy-start.10
  439.3 48.7 %all-gather.11.cloned.1.call-start = ((), (), s32[]{:S(2)}) async-start(), calls=%async_computation.6 | async-start | bytes 22020096 | tf_op jit(solution)/shard_map/all_gather | solution.py:79
  448.6 69.8 %all-gather.9.cloned.1.call-start = ((), (), s32[]{:S(2)}) async-start(), calls=%async_computation.5 | async-start | bytes 22020096 | tf_op jit(solution)/shard_map/all_gather | solution.py:78
  518.4 15.0 %copy-start = (bf16[2048,3584]{1,0:T(8,128)(2,1)S(1)}, bf16[2048,3584]{1,0:T(8,128)(2,1)}, u32[]{:S(2)}) copy-start(bf16[2048,3584]{1,0:T(8,128)(2,1)} %all-gather.11.cloned.1.call-done) | copy-start | bytes 44040196
Sparse Core Ops, SparseCore 0:
  59.3 54.4 all-reduce.3
  117.7 44.7 all-reduce.5
  334.8 48.2 reduce-scatter.3
  385.6 48.7 all-gather.6
  439.4 18.2 all-gather.12
  459.7 28.1 all-gather.10
  490.2 28.1 all-gather.8
where the time goes:
time: 551 us; the launch traced here: 546 us
  waiting for transfers between devices  213 us (39%)
  other arithmetic  155 us (28%)
  local copies, waits for them, and re-layouts  57.9 us (11%)
  matrix products  51.2 us (9%)
  blocking collectives  41.5 us (8%)
  between operations  17.2 us (3%)
  starting transfers between devices  9.69 us (2%)
    another operation x14, other arithmetic, power_step(): factor = jnp.linalg.cholesky(gram_matrix)  80.5 us
    psum x1, waiting for transfers between devices, power_step(): lax.psum(partial_value.astype(jnp.bfloat16), 'tensor').astype(jnp.float32)  54.6 us
    unnamed x8, waiting for transfers between devices  48.4 us
    unnamed x37, local copies, waits for them, and re-layouts  43.8 us
    psum x1, waiting for transfers between devices, power_step(): lax.psum(gram_local.astype(jnp.bfloat16), 'fsdp').astype(jnp.float32)  43.5 us
    another operation x3, other arithmetic, solve_one(): jax.scipy.linalg.solve_triangular(lower_mat, rows_mat.T, lower=True)  42.7 us
    psum x1, blocking collectives, full_back(): lax.psum(jnp.sum(back_piece * back_piece, axis=0), ('fsdp', 'tensor'))  41.5 us
    all_gather x1, waiting for transfers between devices, shards(): lax.all_gather(outputs[0], 'replica', axis=0, tiled=True)  30.4 us
  transfers between devices with their start and end apart: 8, of which 7 were waited for; matrix products, arithmetic and copies ran while one was open for 6% of the time, Pallas kernels for 0%

commit v1 on v0

v1 whole, which is shorter than its diff:
```python
import functools
import math

import jax
import jax.numpy as jnp
from jax import lax
from jax.experimental import pallas as pl
from jax.experimental.pallas import tpu as pltpu
from jax.sharding import PartitionSpec as P

LANES = 128
SUBS = 8
TILE = 512
momentum_decay = 0.95


def invert_block(rows):
    count = len(rows)
    lane = lax.broadcasted_iota(jnp.int32, (SUBS, LANES), 1)
    sub = lax.broadcasted_iota(jnp.int32, (SUBS, LANES), 0)
    rows = list(rows)
    wide = lambda v, i: jnp.broadcast_to(v[i:i+1, :], (SUBS, LANES))
    col = lambda v, c: jnp.broadcast_to(v[:, c:c+1], (SUBS, LANES))
    for p in range(count):
        base = p * SUBS
        inside = (lane >= base) & (lane < base + SUBS)
        mine = rows[p]
        cols = [col(mine, base + i) for i in range(SUBS)]
        solved = jnp.where(inside, jnp.where(lane == base + sub, 1.0, 0.0), mine)
        half = solved
        for i in range(SUBS):
            pivot = wide(cols[i], i)
            inverse = 1.0 / pivot
            at = sub == i
            gain = jnp.where(at, 1.0 - inverse, cols[i] * inverse)
            for j in range(i + 1, SUBS):
                cols[j] = cols[j] - gain * wide(cols[j], i)
            row = wide(solved, i)
            half = jnp.where(at, row * lax.rsqrt(pivot), half)
            solved = solved - gain * row
        rows[p] = jnp.where(lane < base + SUBS, half, 0.0)
        if p + 1 < count:
            wides = [wide(solved, i) for i in range(SUBS)]
            for q in range(p + 1, count):
                below = rows[q]
                terms = [col(below, base + i) * wides[i] for i in range(SUBS)]
                while len(terms) > 1:
                    terms = [a + b for a, b in zip(terms[::2], terms[1::2])]
                rows[q] = jnp.where(inside, 0.0, below) - terms[0]
    return rows


def chol_kernel(gram_ref, hi_ref, lo_ref, work, part):
    blocks = gram_ref.shape[0] // LANES
    for c in range(blocks):
        work[c] = gram_ref[:, c * LANES:(c + 1) * LANES]
    dot = functools.partial(lax.dot_general, preferred_element_type=jnp.float32, precision=lax.Precision.HIGHEST)

    def step(k, carry):
        start = pl.multiple_of(k * LANES, LANES)
        rows = [work[k, pl.ds(start + SUBS * q, SUBS), :] for q in range(LANES // SUBS)]
        inv = jnp.concatenate(invert_block(rows), axis=0)
        for c in range(blocks):
            part[c] = dot(inv, work[c, pl.ds(start, LANES), :], (((1,), (0,)), ((), ())))
        part[k] = inv
        for c in range(blocks):
            work[c, pl.ds(start, LANES), :] = part[c]
        for r in range(1, blocks):
            @pl.when(r > k)
            def _():
                work[k, r * LANES:(r + 1) * LANES, :] = jnp.zeros((LANES, LANES), jnp.float32)
                left = part[r]
                for c in range(blocks):
                    work[c, r * LANES:(r + 1) * LANES, :] -= dot(left, part[c], (((0,), (0,)), ((), ())))
        return carry

    lax.fori_loop(0, blocks, step, 0)
    row = lax.broadcasted_iota(jnp.int32, gram_ref.shape, 0)
    lane = lax.broadcasted_iota(jnp.int32, gram_ref.shape, 1)
    for c in range(blocks):
        cut = slice(c * LANES, (c + 1) * LANES)
        value = jnp.where(row[:, cut] >= lane[:, cut], work[c], 0.0)
        high = value.astype(jnp.bfloat16)
        hi_ref[:, cut] = high
        lo_ref[:, cut] = (value - high.astype(jnp.float32)).astype(jnp.bfloat16)


def inverse_factor(gram):
    n = gram.shape[0]
    return pl.pallas_call(
        chol_kernel,
        out_shape=[jax.ShapeDtypeStruct((n, n), jnp.bfloat16)] * 2,
        in_specs=[pl.BlockSpec(memory_space=pltpu.VMEM)],
        out_specs=[pl.BlockSpec(memory_space=pltpu.VMEM)] * 2,
        scratch_shapes=[pltpu.VMEM((n // LANES, n, LANES), jnp.float32), pltpu.VMEM((n // LANES, LANES, LANES), jnp.float32)],
        compiler_params=pltpu.CompilerParams(vmem_limit_bytes=32 << 20),
        name="inverse_factor",
    )(gram)


def tile_of(size):
    return TILE if size % TILE == 0 else size


def partial_kernel(which_ref, grads_ref, *refs, with_moment):
    if with_moment:
        moment_ref, basis_ref, out_ref, total = refs
        rows = (grads_ref[...].astype(jnp.float32) + moment_ref[...].astype(jnp.float32)).astype(jnp.bfloat16)
    else:
        basis_ref, out_ref, total = refs
        rows = grads_ref[...]
    step = pl.program_id(0)
    product = jnp.dot(rows, basis_ref[...], preferred_element_type=jnp.float32)

    @pl.when(step == 0)
    def _():
        total[...] = product

    @pl.when(step > 0)
    def _():
        total[...] += product

    @pl.when(step == pl.num_programs(0) - 1)
    def _():
        out_ref[...] = total[...].astype(out_ref.dtype)


def partial_projection(which, grads, moment, basis):
    _, rows, units = grads.shape
    rank = basis.shape[-1]
    tile = tile_of(units)
    columns = pl.BlockSpec((None, rows, tile), lambda step, which_ref: (which_ref[0], 0, step))
    factors = pl.BlockSpec((None, tile, rank), lambda step, which_ref: (which_ref[0], step, 0))
    wide = [grads] if moment is None else [grads, moment]
    return pl.pallas_call(
        functools.partial(partial_kernel, with_moment=moment is not None),
        grid_spec=pltpu.PrefetchScalarGridSpec(
            num_scalar_prefetch=1,
            grid=(units // tile,),
            in_specs=[columns] * len(wide) + [factors],
            out_specs=pl.BlockSpec((rows, rank), lambda step, which_ref: (0, 0)),
            scratch_shapes=[pltpu.VMEM((rows, rank), jnp.float32)],
        ),
        out_shape=jax.ShapeDtypeStruct((rows, rank), jnp.bfloat16),
        compiler_params=pltpu.CompilerParams(vmem_limit_bytes=48 << 20),
        name="partial_projection",
    )(which, *wide, basis)


def output_kernel(which_ref, left_ref, back_ref, inverse_ref, blended_ref, *refs, scale):
    momentum_ref, update_ref, basis_ref = refs[-3:]
    dims = (((1,), (1,)), ((), ()))
    left = left_ref[...]
    back = back_ref[...]
    feedback = lax.dot_general(left, back, dims, preferred_element_type=jnp.float32)
    momentum_ref[...] = (blended_ref[...].astype(jnp.float32) - (1.0 - momentum_decay) * feedback).astype(jnp.bfloat16)
    normed = (back.astype(jnp.float32) * inverse_ref[...]).astype(jnp.bfloat16)
    basis_ref[...] = normed
    update_ref[...] = (scale * lax.dot_general(left, normed, dims, preferred_element_type=jnp.float32)).astype(jnp.bfloat16)


def write_outputs(which, left, back, inverse, blended, earlier, scale):
    rows, units = blended.shape
    rank = left.shape[1]
    tile = tile_of(units)
    columns = pl.BlockSpec((None, rows, tile), lambda step, which_ref: (which_ref[0], 0, step))
    return pl.pallas_call(
        functools.partial(output_kernel, scale=scale),
        grid_spec=pltpu.PrefetchScalarGridSpec(
            num_scalar_prefetch=1,
            grid=(units // tile,),
            in_specs=[
                pl.BlockSpec((rows, rank), lambda step, which_ref: (0, 0)),
                pl.BlockSpec((tile, rank), lambda step, which_ref: (step, 0)),
                pl.BlockSpec((1, rank), lambda step, which_ref: (0, 0)),
                pl.BlockSpec((rows, tile), lambda step, which_ref: (0, step)),
            ]
            + [pl.BlockSpec(memory_space=pl.ANY)] * len(earlier),
            out_specs=[
                columns,
                columns,
                pl.BlockSpec((None, tile, rank), lambda step, which_ref: (which_ref[0], step, 0)),
            ],
        ),
        out_shape=[
            jax.ShapeDtypeStruct((2, rows, units), jnp.bfloat16),
            jax.ShapeDtypeStruct((2, rows, units), jnp.bfloat16),
            jax.ShapeDtypeStruct((2, units, rank), jnp.bfloat16),
        ],
        input_output_aliases={5 + i: i for i in range(len(earlier))},
        compiler_params=pltpu.CompilerParams(vmem_limit_bytes=48 << 20),
        name="write_outputs",
    )(which, left, back, inverse, blended, *earlier)


def swap(value, axis, bit, size):
    return lax.ppermute(value, axis, [(i, i ^ bit) for i in range(size)])


def bits_of(size):
    return [1 << i for i in range(size.bit_length() - 1)]


def added(first, second):
    return (first.astype(jnp.float32) + second.astype(jnp.float32)).astype(first.dtype)


def halved(value, axis, bit):
    high = (lax.axis_index(axis) & bit) != 0
    size = value.shape[0] // 2
    first, second = value[:size], value[size:]
    return jnp.where(high, second, first), jnp.where(high, first, second)


def joined(mine, theirs, axis, bit):
    high = (lax.axis_index(axis) & bit) != 0
    return jnp.where(high, jnp.concatenate([theirs, mine]), jnp.concatenate([mine, theirs]))


def reduce_all(values, axis, size, orders):
    values = list(values)
    steps = len(orders[0])
    for step in range(steps):
        for i, order in enumerate(orders):
            keep, send = halved(values[i], axis, order[step])
            values[i] = added(keep, swap(send, axis, order[step], size))
    for step in reversed(range(steps)):
        for i, order in enumerate(orders):
            values[i] = joined(values[i], swap(values[i], axis, order[step], size), axis, order[step])
    return values


def double_all(values, axis, size, orders):
    values = list(values)
    for step in range(len(orders[0])):
        for i, order in enumerate(orders):
            values[i] = added(values[i], swap(values[i], axis, order[step], size))
    return values


def times_inverse(rows, high, low):
    dims = (((1,), (1,)), ((), ()))
    return lax.dot_general(rows, high, dims, preferred_element_type=jnp.float32) + lax.dot_general(
        rows, low, dims, preferred_element_type=jnp.float32
    )


def shards(grads, momentum, basis, *, sizes):
    owner = lax.axis_index("replica")
    own = owner.astype(jnp.int32).reshape(1)
    other = 1 - own
    grads = grads[0]
    fsdp, tensor = sizes["fsdp"], sizes["tensor"]
    bits = bits_of(fsdp)
    orders = [bits, bits[::-1]]

    sent = partial_projection(other, grads, None, basis)
    received = swap(sent, "replica", 1, 2)
    mine = partial_projection(own, grads, momentum, basis)
    (projected,) = reduce_all([added(mine, received)], "tensor", tensor, [bits_of(tensor)])

    theirs = swap(lax.dynamic_index_in_dim(grads, other[0], 0, keepdims=False), "replica", 1, 2)
    total = lax.dynamic_index_in_dim(grads, owner, 0, keepdims=False).astype(jnp.float32) + theirs.astype(jnp.float32)
    blended = (lax.dynamic_index_in_dim(momentum, owner, 0, keepdims=False).astype(jnp.float32) + total).astype(
        jnp.bfloat16
    )
    blended_other = swap(blended, "replica", 1, 2)

    gram = lax.dot_general(
        projected, projected, (((0,), (0,)), ((), ())), preferred_element_type=jnp.float32
    ).astype(jnp.bfloat16)
    half = gram.shape[0] // 2
    gram = jnp.concatenate(double_all([gram[:half], gram[half:]], "fsdp", fsdp, orders))
    high, low = inverse_factor(gram.astype(jnp.float32))

    crossed = lax.dot_general(
        blended, projected, (((0,), (0,)), ((), ())), preferred_element_type=jnp.float32
    ).astype(jnp.bfloat16)
    half = crossed.shape[0] // 2
    crossed = jnp.concatenate(reduce_all([crossed[:half], crossed[half:]], "fsdp", fsdp, orders))

    left = times_inverse(projected, high, low).astype(jnp.bfloat16)
    back = times_inverse(crossed, high, low)
    squares = jnp.sum(back * back, axis=0, keepdims=True)
    (squares,) = double_all([squares], "tensor", tensor, [bits_of(tensor)])
    back = back.astype(jnp.bfloat16)
    inverse = 1.0 / (jnp.sqrt(squares) + 1e-06)
    left_other = swap(left, "replica", 1, 2)
    back_other = swap(back, "replica", 1, 2)
    inverse_other = swap(inverse, "replica", 1, 2)

    scale = math.sqrt(grads.shape[1] * fsdp * grads.shape[2] * tensor / basis.shape[-1])
    outputs = write_outputs(own, left, back, inverse, blended, (), scale)
    return tuple(write_outputs(other, left_other, back_other, inverse_other, blended_other, outputs, scale))


def solution(mesh):
    placed = (
        P("replica", None, "fsdp", "tensor"),
        P(None, "fsdp", "tensor"),
        P(None, "tensor", None),
    )
    return jax.shard_map(
        functools.partial(shards, sizes=dict(mesh.shape)),
        mesh=mesh,
        in_specs=placed,
        out_specs=(P(None, "fsdp", "tensor"), P(None, "fsdp", "tensor"), P(None, "tensor", None)),
        check_vma=False,
    )
```

time: 551 us -> 241 us (0.44)
  other arithmetic: 155 us -> 15.3 us
  waiting for transfers between devices: 213 us -> 105 us
  Pallas kernels: 0 us -> 70.3 us
  local copies, waits for them, and re-layouts: 57.9 us -> 6.64 us
  blocking collectives: 41.5 us -> 0 us
  matrix products: 51.2 us -> 17.5 us
  between operations: 17.2 us -> 0.94 us
  starting transfers between devices: 9.69 us -> 24.4 us
    another operation x17 -> x0, other arithmetic: 123 us -> none  [the longest x14 80.5 us: power_step(): factor = jnp.linalg.cholesky(gram_matrix)]
    ppermute x0 -> x24, waiting for transfers between devices: none -> 105 us  [swap(): return lax.ppermute(value, axis, [(i, i ^ bit) for i in range(size)])]
    psum x2 -> x0, waiting for transfers between devices: 98.1 us -> none  [the longest x1 54.6 us: power_step(): lax.psum(partial_value.astype(jnp.bfloat16), 'tensor').astype(jnp.float32)]
    pallas_call x0 -> x5, Pallas kernels: none -> 70.3 us  [the longest x2 27 us: write_outputs(): pl.pallas_call(functools.partial(output_kernel, scale=scale), grid_spec=p...]
    all_gather x4 -> x0, waiting for transfers between devices: 54.8 us -> none  [the longest x1 30.4 us: shards(): lax.all_gather(outputs[0], 'replica', axis=0, tiled=True)]
    unnamed x8 -> x0, waiting for transfers between devices: 48.4 us -> none
    unnamed x37 -> x0, local copies, waits for them, and re-layouts: 43.8 us -> none
    psum x1 -> x0, blocking collectives: 41.5 us -> none  [full_back(): lax.psum(jnp.sum(back_piece * back_piece, axis=0), ('fsdp', 'tensor'))]
  transfers between devices with their start and end apart: 8 -> 24, of which waited for: 7 -> 14; matrix products, arithmetic and copies ran while one was open for 6% -> 10% of each run, Pallas kernels for 0% -> 24%
where the time goes in v1:
time: 241 us; the launch traced here: 240 us
  waiting for transfers between devices  105 us (44%)
  Pallas kernels  70.3 us (29%)
  starting transfers between devices  24.4 us (10%)
  matrix products  17.5 us (7%)
  other arithmetic  15.3 us (6%)
  local copies, waits for them, and re-layouts  6.64 us (3%)
    ppermute x24, waiting for transfers between devices, swap(): return lax.ppermute(value, axis, [(i, i ^ bit) for i in range(size)])  105 us
    pallas_call x2, Pallas kernels, write_outputs(): pl.pallas_call(functools.partial(output_kernel, scale=scale), grid_spec=p...  27 us
    ppermute x24, starting transfers between devices, swap(): return lax.ppermute(value, axis, [(i, i ^ bit) for i in range(size)])  24.4 us
    pallas_call x1, Pallas kernels, inverse_factor(): pl.pallas_call(chol_kernel, out_shape=[jax.ShapeDtypeStruct((n, n), jnp.b...  23.5 us
    pallas_call x2, Pallas kernels, partial_projection(): pl.pallas_call(functools.partial(partial_kernel, with_moment=moment is no...  19.8 us
    convert_element_type x1, other arithmetic, shards(): (lax.dynamic_index_in_dim(momentum, owner, 0, keepdims=False).astype(jnp....  10.8 us
    dot_general x1, matrix products, shards(): lax.dot_general(blended, projected, (((0,), (0,)), ((), ())), preferred_e...  7.39 us
    squeeze x1, local copies, waits for them, and re-layouts, shards(): lax.dynamic_index_in_dim(grads, other[0], 0, keepdims=False)  6.61 us
  transfers between devices with their start and end apart: 24, of which 14 were waited for; matrix products, arithmetic and copies ran while one was open for 10% of the time, Pallas kernels for 24%

profile of v1, /device:TPU:0, one launch (start us, length us, event | category | flops | bytes accessed | tf_op | source)
XLA Modules:
  0.0 240.2 jit_solution(12881632045365103989)
XLA Ops:
  0.6 6.6 %dynamic-slice_bitcast_fusion = bf16[1024,3584]{1,0:T(8,128)(2,1)} fusion(bf16[1,2,1024,3584]{3,2,1,0:T(8,128)(2,1)} %param.3, s32[]{:T(128)S(6)} %select_n.127), kind=kLoop, calls=%fused_computation.4 | loop fusion | bytes 14680068 | tf_op jit(solution)/shard_map/jit(dynamic_index_in_dim)/squeeze | solution.py:262
  7.7 9.2 %partial_projection.3 = bf16[1024,512]{1,0:T(8,128)(2,1)S(1)} custom-call(s32[1]{0:T(128)} %sub.3.which_ref, bf16[2,1024,3584]{2,1,0:T(8,128)(2,1)} %bitcast.17, bf16[2,3584,512]{2,1,0:T(8,128)(2,1)} %refs_0_.3), custom_call_target="tpu_custom_call" | custom-call | tf_op jit(solution)/shard_map/partial_projection/pallas_call | solution.py:135
  17.0 10.6 %partial_projection.2 = bf16[1024,512]{1,0:T(8,128)(2,1)S(1)} custom-call(s32[1]{0:T(128)} %bitcast.which_ref, bf16[2,1024,3584]{2,1,0:T(8,128)(2,1)} %bitcast.18, bf16[2,1024,3584]{2,1,0:T(8,128)(2,1)} %refs_0_.2, bf16[2,3584,512]{2,1,0:T(8,128)(2,1)} %refs_0_.3), custom_call_target="tpu_custom_call" | custom-call | tf_op jit(solution)/shard_map/partial_projection/pallas_call | solution.py:135
  28.0 3.1 %collective-permute-start.1 = (bf16[512,512]{1,0:T(8,128)(2,1)S(1)}, bf16[512,512]{1,0:T(8,128)(2,1)S(1)}, u32[]{:S(2)}, u32[]{:S(2)}) collective-permute-start(bf16[512,512]{1,0:T(8,128)(2,1)S(1)} %broadcast_select_fusion.2), channel_id=1, source_target_pairs={{0,1},{1,0},{2,3},{3,2},{4,5},{5,4},{6,7},{7,6},{8,9},{9,8},{10,11... | collective-permute-start | bytes 1572872 | tf_op jit(solution)/shard_map/ppermute | solution.py:197
  31.1 12.1 %collective-permute-done.1 = bf16[512,512]{1,0:T(8,128)(2,1)S(1)} collective-permute-done((bf16[512,512]{1,0:T(8,128)(2,1)S(1)}, bf16[512,512]{1,0:T(8,128)(2,1)S(1)}, u32[]{:S(2)}, u32[]{:S(2)}) %collective-permute-start.1) | collective-permute-done | bytes 524320 | tf_op jit(solution)/shard_map/ppermute | solution.py:197
  43.5 2.8 %collective-permute-start.2 = (bf16[256,512]{1,0:T(8,128)(2,1)S(1)}, bf16[256,512]{1,0:T(8,128)(2,1)S(1)}, u32[]{:S(2)}, u32[]{:S(2)}) collective-permute-start(bf16[256,512]{1,0:T(8,128)(2,1)S(1)} %broadcast_select_fusion.5), channel_id=1, source_target_pairs={{0,2},{1,3},{2,0},{3,1},{4,6},{5,7},{6,4},{7,5},{8,10},{9,11},{10,... | collective-permute-start | bytes 786440 | tf_op jit(solution)/shard_map/ppermute | solution.py:197
  46.3 11.5 %collective-permute-done.2 = bf16[256,512]{1,0:T(8,128)(2,1)S(1)} collective-permute-done((bf16[256,512]{1,0:T(8,128)(2,1)S(1)}, bf16[256,512]{1,0:T(8,128)(2,1)S(1)}, u32[]{:S(2)}, u32[]{:S(2)}) %collective-permute-start.2) | collective-permute-done | bytes 262176 | tf_op jit(solution)/shard_map/ppermute | solution.py:197
  58.0 13.8 %collective-permute-done.3 = bf16[256,512]{1,0:T(8,128)(2,1)S(1)} collective-permute-done((bf16[256,512]{1,0:T(8,128)(2,1)S(1)}, bf16[256,512]{1,0:T(8,128)(2,1)S(1)}, u32[]{:S(2)}, u32[]{:S(2)}) %collective-permute-start.3) | collective-permute-done | bytes 262176 | tf_op jit(solution)/shard_map/ppermute | solution.py:197
  72.1 10.8 %fusion.1.blended_ref = bf16[1024,3584]{1,0:T(8,128)(2,1)} fusion(bf16[1024,3584]{1,0:T(8,128)(2,1)} %collective-permute-done.10, bf16[1,2,1024,3584]{3,2,1,0:T(8,128)(2,1)} %param.3, s32[]{:T(128)S(6)} %select_n.126, bf16[2,1024,3584]{2,1,0:T(8,128)(2,1)} %refs_0_.2), kind=kLoop, calls=%fused_computation.2 | loop fusion | flops 22020096 | bytes 29360132 | tf_op jit(solution)/shard_map/convert_element_type | solution.py:264
  82.8 1.4 collective-permute-done.4
  84.2 7.4 %convolution_convert_fusion = bf16[3584,512]{1,0:T(8,128)(2,1)S(1)} fusion(bf16[1024,3584]{1,0:T(8,128)(2,1)} %fusion.1.blended_ref, bf16[512,512]{1,0:T(8,128)(2,1)S(1)} %maximum_select_fusion.5, bf16[512,512]{1,0:T(8,128)(2,1)S(1)} %collective-permute-done.4, pred[]{:T(512)S(6)} %ne.8), kind=kOutput, calls=%fused_computation.6 | convolution fusion | flops 3764649984 | bytes 12058625 | tf_op jit(solution)/shard_map/dot_general | solution.py:276
  92.8 1.4 collective-permute-start.15
  94.2 17.3 %collective-permute-done.11 = bf16[896,512]{1,0:T(8,128)(2,1)S(1)} collective-permute-done((bf16[896,512]{1,0:T(8,128)(2,1)S(1)}, bf16[896,512]{1,0:T(8,128)(2,1)S(1)}, u32[]{:S(2)}, u32[]{:S(2)}) %collective-permute-start.11) | collective-permute-done | bytes 917536 | tf_op jit(solution)/shard_map/ppermute | solution.py:197
  113.1 1.6 collective-permute-start.12
  116.1 7.5 %collective-permute-done.12 = bf16[448,512]{1,0:T(8,128)(2,1)S(1)} collective-permute-done((bf16[448,512]{1,0:T(8,128)(2,1)S(1)}, bf16[448,512]{1,0:T(8,128)(2,1)S(1)}, u32[]{:S(2)}, u32[]{:S(2)}) %collective-permute-start.12) | collective-permute-done | bytes 458784 | tf_op jit(solution)/shard_map/ppermute | solution.py:197
  123.8 2.0 collective-permute-start.13
  125.9 1.3 collective-permute-start.7
  127.2 1.8 collective-permute-done.16
  129.7 4.7 %collective-permute-done.13 = bf16[448,512]{1,0:T(8,128)(2,1)S(1)} collective-permute-done((bf16[448,512]{1,0:T(8,128)(2,1)S(1)}, bf16[448,512]{1,0:T(8,128)(2,1)S(1)}, u32[]{:S(2)}, u32[]{:S(2)}) %collective-permute-start.13) | collective-permute-done | bytes 458784 | tf_op jit(solution)/shard_map/ppermute | solution.py:197
  134.8 1.4 collective-permute-start.14
  136.2 1.9 collective-permute-done.7
  138.2 2.1 collective-permute-start.6
  140.3 4.6 %collective-permute-done.17 = bf16[448,512]{1,0:T(8,128)(2,1)S(1)} collective-permute-done((bf16[448,512]{1,0:T(8,128)(2,1)S(1)}, bf16[448,512]{1,0:T(8,128)(2,1)S(1)}, u32[]{:S(2)}, u32[]{:S(2)}) %collective-permute-start.17) | collective-permute-done | bytes 458784 | tf_op jit(solution)/shard_map/ppermute | solution.py:197
  145.6 23.7 %collective-permute-done.8 = bf16[256,512]{1,0:T(8,128)(2,1)S(1)} collective-permute-done((bf16[256,512]{1,0:T(8,128)(2,1)S(1)}, bf16[256,512]{1,0:T(8,128)(2,1)S(1)}, u32[]{:S(2)}, u32[]{:S(2)}) %collective-permute-start.8) | collective-permute-done | bytes 262176 | tf_op jit(solution)/shard_map/ppermute | solution.py:197
  169.5 23.5 %inverse_factor.1 = (bf16[512,512]{1,0:T(8,128)(2,1)S(1)}, bf16[512,512]{1,0:T(8,128)(2,1)S(1)}) custom-call(f32[512,512]{1,0:T(8,128)S(1)} %maximum_convert_fusion.gram_ref), custom_call_target="tpu_custom_call" | custom-call | tf_op jit(solution)/shard_map/inverse_factor/pallas_call | solution.py:90
  194.1 2.3 fusion.2
  196.3 5.6 %multiply_reduce_fusion = (f32[512]{0:T(512)S(1)}, bf16[3584,512]{1,0:T(8,128)(2,1)S(1)}) fusion(f32[3584,512]{1,0:T(8,128)S(1)} %fusion.2, bf16[512,512]{1,0:T(8,128)(2,1)S(1)} %get-tuple-element.9, bf16[1792,512]{1,0:T(8,128)(2,1)S(1)} %maximum_select_fusion.1, bf16[1792,512]{1,0:T(8,128)(2,1)S(1)} %maximum_select_fusion), kind=kOutput, calls=%fused_computation.3 | convolution fusion | flops 1893727744 | bytes 15206400 | tf_op jit(solution)/shard_map/dot_general | solution.py:243
  205.1 2.5 %collective-permute-done.20 = f32[1,512]{1,0:T(1,128)S(1)} collective-permute-done((f32[1,512]{1,0:T(1,128)S(1)}, f32[1,512]{1,0:T(1,128)S(1)}, u32[]{:S(2)}, u32[]{:S(2)}) %collective-permute-start.20) | collective-permute-done | bytes 2080 | tf_op jit(solution)/shard_map/ppermute | solution.py:197
  207.7 3.9 %collective-permute-start.21 = (f32[1,512]{1,0:T(1,128)S(1)}, f32[1,512]{1,0:T(1,128)S(1)}, u32[]{:S(2)}, u32[]{:S(2)}) collective-permute-start(f32[1,512]{1,0:T(1,128)S(1)} %add.82), channel_id=1, source_target_pairs={{0,2},{1,3},{2,0},{3,1},{4,6},{5,7},{6,4},{7,5},{8,10},{9,11},{10,... | collective-permute-start | bytes 6152 | tf_op jit(solution)/shard_map/ppermute | solution.py:197
  211.5 1.6 collective-permute-done.21
  213.2 13.5 %write_outputs.2 = (bf16[2,1024,3584]{2,1,0:T(8,128)(2,1)}, bf16[2,1024,3584]{2,1,0:T(8,128)(2,1)}, bf16[2,3584,512]{2,1,0:T(8,128)(2,1)}) custom-call(s32[1]{0:T(128)} %bitcast.which_ref, bf16[1024,512]{1,0:T(8,128)(2,1)S(1)} %add_convert_fusion.left_ref, bf16[3584,512]{1,0:T(8,128)(2,1)S(1)} %get-tuple-element.14.back_ref, ...), custom_call_target="tpu_custom_call" | custom-call | tf_op jit(solution)/shard_map/write_outputs/pallas_call | solution.py:167
  226.7 13.5 %write_outputs.3 = (bf16[2,1024,3584]{2,1,0:T(8,128)(2,1)}, bf16[2,1024,3584]{2,1,0:T(8,128)(2,1)}, bf16[2,3584,512]{2,1,0:T(8,128)(2,1)}) custom-call(s32[1]{0:T(128)} %sub.3.which_ref, bf16[1024,512]{1,0:T(8,128)(2,1)S(1)} %collective-permute-done.9.left_ref, ...), custom_call_target="tpu_custom_call", output_to_operand_aliasing={{0}: (5, {}), {1}: (6, {}), {2}: (7, {})} | custom-call | tf_op jit(solution)/shard_map/write_outputs/pallas_call | solution.py:167
  (52 shorter events, 12.4 us)
Async XLA Ops:
  7.2 64.8 %collective-permute-start.10 = (bf16[1024,3584]{1,0:T(8,128)(2,1)}, bf16[1024,3584]{1,0:T(8,128)(2,1)}, u32[]{:S(2)}, u32[]{:S(2)}) collective-permute-start(bf16[1024,3584]{1,0:T(8,128)(2,1)} %dynamic-slice_bitcast_fusion), channel_id=1, source_target_pairs={{0,16},{16,0},{1,17},{17,1},{2,18},{18,2},{3,19},{19,3},{4,20},{20... | collective-permute-start | bytes 22020104 | tf_op jit(solution)/shard_map/ppermute | solution.py:197
  16.9 10.7 %collective-permute-start = (bf16[1024,512]{1,0:T(8,128)(2,1)S(1)}, bf16[1024,512]{1,0:T(8,128)(2,1)S(1)}, u32[]{:S(2)}, u32[]{:S(2)}) collective-permute-start(bf16[1024,512]{1,0:T(8,128)(2,1)S(1)} %partial_projection.3), channel_id=1, source_target_pairs={{0,16},{16,0},{1,17},{17,1},{2,18},{18,2},{3,19},{19,3},{4,20},{20... | collective-permute-start | bytes 3145736 | tf_op jit(solution)/shard_map/ppermute | solution.py:197
  28.0 15.2 %collective-permute-start.1 = (bf16[512,512]{1,0:T(8,128)(2,1)S(1)}, bf16[512,512]{1,0:T(8,128)(2,1)S(1)}, u32[]{:S(2)}, u32[]{:S(2)}) collective-permute-start(bf16[512,512]{1,0:T(8,128)(2,1)S(1)} %broadcast_select_fusion.2), channel_id=1, source_target_pairs={{0,1},{1,0},{2,3},{3,2},{4,5},{5,4},{6,7},{7,6},{8,9},{9,8},{10,11... | collective-permute-start | bytes 1572872 | tf_op jit(solution)/shard_map/ppermute | solution.py:197
  43.5 14.3 %collective-permute-start.2 = (bf16[256,512]{1,0:T(8,128)(2,1)S(1)}, bf16[256,512]{1,0:T(8,128)(2,1)S(1)}, u32[]{:S(2)}, u32[]{:S(2)}) collective-permute-start(bf16[256,512]{1,0:T(8,128)(2,1)S(1)} %broadcast_select_fusion.5), channel_id=1, source_target_pairs={{0,2},{1,3},{2,0},{3,1},{4,6},{5,7},{6,4},{7,5},{8,10},{9,11},{10,... | collective-permute-start | bytes 786440 | tf_op jit(solution)/shard_map/ppermute | solution.py:197
  57.9 13.9 %collective-permute-start.3 = (bf16[256,512]{1,0:T(8,128)(2,1)S(1)}, bf16[256,512]{1,0:T(8,128)(2,1)S(1)}, u32[]{:S(2)}, u32[]{:S(2)}) collective-permute-start(bf16[256,512]{1,0:T(8,128)(2,1)S(1)} %add_convert_fusion.11), channel_id=1, source_target_pairs={{0,2},{1,3},{2,0},{3,1},{4,6},{5,7},{6,4},{7,5},{8,10},{9,11},{10,... | collective-permute-start | bytes 786440 | tf_op jit(solution)/shard_map/ppermute | solution.py:197
  72.0 12.2 %collective-permute-start.4 = (bf16[512,512]{1,0:T(8,128)(2,1)S(1)}, bf16[512,512]{1,0:T(8,128)(2,1)S(1)}, u32[]{:S(2)}, u32[]{:S(2)}) collective-permute-start(bf16[512,512]{1,0:T(8,128)(2,1)S(1)} %maximum_select_fusion.5), channel_id=1, source_target_pairs={{0,1},{1,0},{2,3},{3,2},{4,5},{5,4},{6,7},{7,6},{8,9},{9,8},{10,11... | collective-permute-start | bytes 1572872 | tf_op jit(solution)/shard_map/ppermute | solution.py:197
  91.8 19.7 %collective-permute-start.11 = (bf16[896,512]{1,0:T(8,128)(2,1)S(1)}, bf16[896,512]{1,0:T(8,128)(2,1)S(1)}, u32[]{:S(2)}, u32[]{:S(2)}) collective-permute-start(bf16[896,512]{1,0:T(8,128)(2,1)S(1)} %get-tuple-element.17), channel_id=1, source_target_pairs={{0,4},{4,0},{8,12},{12,8},{1,5},{5,1},{9,13},{13,9},{2,6},{6,2},{1... | collective-permute-start | bytes 2752520 | tf_op jit(solution)/shard_map/ppermute | solution.py:197
  92.8 19.5 %collective-permute-start.15 = (bf16[896,512]{1,0:T(8,128)(2,1)S(1)}, bf16[896,512]{1,0:T(8,128)(2,1)S(1)}, u32[]{:S(2)}, u32[]{:S(2)}) collective-permute-start(bf16[896,512]{1,0:T(8,128)(2,1)S(1)} %get-tuple-element.18), channel_id=1, source_target_pairs={{0,8},{4,12},{8,0},{12,4},{1,9},{5,13},{9,1},{13,5},{2,10},{6,14},... | collective-permute-start | bytes 2752520 | tf_op jit(solution)/shard_map/ppermute | solution.py:197
  113.1 10.5 %collective-permute-start.12 = (bf16[448,512]{1,0:T(8,128)(2,1)S(1)}, bf16[448,512]{1,0:T(8,128)(2,1)S(1)}, u32[]{:S(2)}, u32[]{:S(2)}) collective-permute-start(bf16[448,512]{1,0:T(8,128)(2,1)S(1)} %broadcast_select_fusion.4), channel_id=1, source_target_pairs={{0,8},{4,12},{8,0},{12,4},{1,9},{5,13},{9,1},{13,5},{2,10},{6,14},... | collective-permute-start | bytes 1376264 | tf_op jit(solution)/shard_map/ppermute | solution.py:197
  115.5 111.2 %collective-permute-start.23 = (bf16[1024,3584]{1,0:T(8,128)(2,1)}, bf16[1024,3584]{1,0:T(8,128)(2,1)}, u32[]{:S(2)}, u32[]{:S(2)}) collective-permute-start(bf16[1024,3584]{1,0:T(8,128)(2,1)} %fusion.1.blended_ref), channel_id=1, source_target_pairs={{0,16},{16,0},{1,17},{17,1},{2,18},{18,2},{3,19},{19,3},{4,20},{20... | collective-permute-start | bytes 22020104 | tf_op jit(solution)/shard_map/ppermute | solution.py:197
  115.6 13.4 %collective-permute-start.16 = (bf16[448,512]{1,0:T(8,128)(2,1)S(1)}, bf16[448,512]{1,0:T(8,128)(2,1)S(1)}, u32[]{:S(2)}, u32[]{:S(2)}) collective-permute-start(bf16[448,512]{1,0:T(8,128)(2,1)S(1)} %broadcast_select_fusion.3), channel_id=1, source_target_pairs={{0,4},{4,0},{8,12},{12,8},{1,5},{5,1},{9,13},{13,9},{2,6},{6,2},{1... | collective-permute-start | bytes 1376264 | tf_op jit(solution)/shard_map/ppermute | solution.py:197
  123.8 10.6 %collective-permute-start.13 = (bf16[448,512]{1,0:T(8,128)(2,1)S(1)}, bf16[448,512]{1,0:T(8,128)(2,1)S(1)}, u32[]{:S(2)}, u32[]{:S(2)}) collective-permute-start(bf16[448,512]{1,0:T(8,128)(2,1)S(1)} %add_convert_fusion.6), channel_id=1, source_target_pairs={{0,8},{4,12},{8,0},{12,4},{1,9},{5,13},{9,1},{13,5},{2,10},{6,14},... | collective-permute-start | bytes 1376264 | tf_op jit(solution)/shard_map/ppermute | solution.py:197
  125.8 10.4 %collective-permute-start.5 = (bf16[256,512]{1,0:T(8,128)(2,1)S(1)}, bf16[256,512]{1,0:T(8,128)(2,1)S(1)}, u32[]{:S(2)}, u32[]{:S(2)}) collective-permute-start(bf16[256,512]{1,0:T(8,128)(2,1)S(1)} %get-tuple-element.21), channel_id=1, source_target_pairs={{0,4},{4,0},{8,12},{12,8},{1,5},{5,1},{9,13},{13,9},{2,6},{6,2},{1... | collective-permute-start | bytes 786440 | tf_op jit(solution)/shard_map/ppermute | solution.py:197
  125.9 12.2 %collective-permute-start.7 = (bf16[256,512]{1,0:T(8,128)(2,1)S(1)}, bf16[256,512]{1,0:T(8,128)(2,1)S(1)}, u32[]{:S(2)}, u32[]{:S(2)}) collective-permute-start(bf16[256,512]{1,0:T(8,128)(2,1)S(1)} %get-tuple-element.22), channel_id=1, source_target_pairs={{0,8},{4,12},{8,0},{12,4},{1,9},{5,13},{9,1},{13,5},{2,10},{6,14},... | collective-permute-start | bytes 786440 | tf_op jit(solution)/shard_map/ppermute | solution.py:197
  129.2 15.7 %collective-permute-start.17 = (bf16[448,512]{1,0:T(8,128)(2,1)S(1)}, bf16[448,512]{1,0:T(8,128)(2,1)S(1)}, u32[]{:S(2)}, u32[]{:S(2)}) collective-permute-start(bf16[448,512]{1,0:T(8,128)(2,1)S(1)} %add_convert_fusion.5), channel_id=1, source_target_pairs={{0,4},{4,0},{8,12},{12,8},{1,5},{5,1},{9,13},{13,9},{2,6},{6,2},{1... | collective-permute-start | bytes 1376264 | tf_op jit(solution)/shard_map/ppermute | solution.py:197
  134.8 58.2 %collective-permute-start.14 = (bf16[896,512]{1,0:T(8,128)(2,1)S(1)}, bf16[896,512]{1,0:T(8,128)(2,1)S(1)}, u32[]{:S(2)}, u32[]{:S(2)}) collective-permute-start(bf16[896,512]{1,0:T(8,128)(2,1)S(1)} %maximum_select_fusion.3), channel_id=1, source_target_pairs={{0,4},{4,0},{8,12},{12,8},{1,5},{5,1},{9,13},{13,9},{2,6},{6,2},{1... | collective-permute-start | bytes 2752520 | tf_op jit(solution)/shard_map/ppermute | solution.py:197
  138.2 7.3 %collective-permute-start.6 = (bf16[256,512]{1,0:T(8,128)(2,1)S(1)}, bf16[256,512]{1,0:T(8,128)(2,1)S(1)}, u32[]{:S(2)}, u32[]{:S(2)}) collective-permute-start(bf16[256,512]{1,0:T(8,128)(2,1)S(1)} %get-tuple-element.19), channel_id=1, source_target_pairs={{0,8},{4,12},{8,0},{12,4},{1,9},{5,13},{9,1},{13,5},{2,10},{6,14},... | collective-permute-start | bytes 786440 | tf_op jit(solution)/shard_map/ppermute | solution.py:197
  140.3 29.0 %collective-permute-start.8 = (bf16[256,512]{1,0:T(8,128)(2,1)S(1)}, bf16[256,512]{1,0:T(8,128)(2,1)S(1)}, u32[]{:S(2)}, u32[]{:S(2)}) collective-permute-start(bf16[256,512]{1,0:T(8,128)(2,1)S(1)} %get-tuple-element.20), channel_id=1, source_target_pairs={{0,4},{4,0},{8,12},{12,8},{1,5},{5,1},{9,13},{13,9},{2,6},{6,2},{1... | collective-permute-start | bytes 786440 | tf_op jit(solution)/shard_map/ppermute | solution.py:197
  145.3 48.2 %collective-permute-start.18 = (bf16[896,512]{1,0:T(8,128)(2,1)S(1)}, bf16[896,512]{1,0:T(8,128)(2,1)S(1)}, u32[]{:S(2)}, u32[]{:S(2)}) collective-permute-start(bf16[896,512]{1,0:T(8,128)(2,1)S(1)} %maximum_select_fusion.4), channel_id=1, source_target_pairs={{0,8},{4,12},{8,0},{12,4},{1,9},{5,13},{9,1},{13,5},{2,10},{6,14},... | collective-permute-start | bytes 2752520 | tf_op jit(solution)/shard_map/ppermute | solution.py:197
  201.9 24.7 %collective-permute-start.19 = (bf16[3584,512]{1,0:T(8,128)(2,1)S(1)}, bf16[3584,512]{1,0:T(8,128)(2,1)S(1)}, u32[]{:S(2)}, u32[]{:S(2)}) collective-permute-start(bf16[3584,512]{1,0:T(8,128)(2,1)S(1)} %get-tuple-element.14.back_ref), channel_id=1, source_target_pairs={{0,16},{16,0},{1,17},{17,1},{2,18},{18,2},{3,19},{19,3},{4,20},{20... | collective-permute-start | bytes 11010056 | tf_op jit(solution)/shard_map/ppermute | solution.py:197
  203.5 23.1 %collective-permute-start.9 = (bf16[1024,512]{1,0:T(8,128)(2,1)S(1)}, bf16[1024,512]{1,0:T(8,128)(2,1)S(1)}, u32[]{:S(2)}, u32[]{:S(2)}) collective-permute-start(bf16[1024,512]{1,0:T(8,128)(2,1)S(1)} %add_convert_fusion.left_ref), channel_id=1, source_target_pairs={{0,16},{16,0},{1,17},{17,1},{2,18},{18,2},{3,19},{19,3},{4,20},{20... | collective-permute-start | bytes 3145736 | tf_op jit(solution)/shard_map/ppermute | solution.py:197
  204.1 3.6 %collective-permute-start.20 = (f32[1,512]{1,0:T(1,128)S(1)}, f32[1,512]{1,0:T(1,128)S(1)}, u32[]{:S(2)}, u32[]{:S(2)}) collective-permute-start(f32[1,512]{1,0:T(1,128)S(1)} %bitcast.19), channel_id=1, source_target_pairs={{0,1},{1,0},{2,3},{3,2},{4,5},{5,4},{6,7},{7,6},{8,9},{9,8},{10,11... | collective-permute-start | bytes 6152 | tf_op jit(solution)/shard_map/ppermute | solution.py:197
  207.7 5.4 %collective-permute-start.21 = (f32[1,512]{1,0:T(1,128)S(1)}, f32[1,512]{1,0:T(1,128)S(1)}, u32[]{:S(2)}, u32[]{:S(2)}) collective-permute-start(f32[1,512]{1,0:T(1,128)S(1)} %add.82), channel_id=1, source_target_pairs={{0,2},{1,3},{2,0},{3,1},{4,6},{5,7},{6,4},{7,5},{8,10},{9,11},{10,... | collective-permute-start | bytes 6152 | tf_op jit(solution)/shard_map/ppermute | solution.py:197
  213.1 13.6 %collective-permute-start.22 = (f32[1,512]{1,0:T(1,128)S(1)}, f32[1,512]{1,0:T(1,128)S(1)}, u32[]{:S(2)}, u32[]{:S(2)}) collective-permute-start(f32[1,512]{1,0:T(1,128)S(1)} %add_divide_fusion.inverse_ref), channel_id=1, source_target_pairs={{0,16},{16,0},{1,17},{17,1},{2,18},{18,2},{3,19},{19,3},{4,20},{20... | collective-permute-start | bytes 6152 | tf_op jit(solution)/shard_map/ppermute | solution.py:197
